TPU v7x, 256 devices: a whole 4x4x8 slice. The times are simulated.
256 devices in a mesh: dp: 4 (over y), gx: 4 (over x), gy: 16 (over z, core).
Axes of the slice: x: 4, y: 4, z: 8, core: 2. Of those that a mesh axis runs over, the one named last changes fastest.
Arguments:
- field: bfloat16 [4, 64, 32, 20, 2048], P('dp', 'gx', 'gy'), may hold values from -6 to 6
- cotangent: bfloat16 [4, 64, 32, 20, 2048], P('dp', 'gx', 'gy'), may hold values from -6 to 6
- spectral_weight: bfloat16 [24, 24, 20, 20, 192], P(None, None, None, None, ('gx', 'gy')), may hold values from -2.5 to 2.5
- bypass_weight: bfloat16 [20, 20], replicated, may hold values from -1.25 to 1.25
Outputs:
- grad_field: bfloat16 [4, 64, 32, 20, 2048], P('dp', 'gx', 'gy')
- grad_spectral: float32 [24, 24, 20, 20, 192], P(None, None, None, None, ('gx', 'gy'))
- grad_bypass: float32 [20, 20], replicated
All inputs are finite; a program needn't handle non-finite values.
Results may differ from a plain program's by a relative error of at most 0.034.
Values may be sent and summed in bfloat16 or wider, within the bound.
No kernel may reach another device: no remote copies, remote signals or barrier semaphores. Data moves between devices by JAX's collectives and lax.ppermute only.
A program may use at most 192 MiB of HBM per device.

v0:
```python
import math
import jax
import jax.numpy as jnp
from jax import lax
from jax.sharding import PartitionSpec as P

MX = 12
MY = 12
MZ = 12
MT = 4
NZ = 128
NT = 16


def basis(length, kept):
    places = lax.iota(jnp.int32, length)
    orders = lax.iota(jnp.int32, kept)
    cos_arg = places[:, None] * orders[None, :] % length
    sin_arg = places[:, None] * (orders[None, :] + 1) % length
    step_angle = 2.0 * math.pi / length
    scale = math.sqrt(2.0 / length)
    cos_part = jnp.cos(cos_arg.astype(jnp.float32) * step_angle)
    sin_part = jnp.sin(sin_arg.astype(jnp.float32) * step_angle)
    return jnp.concatenate([cos_part, sin_part], axis=1) * scale


def mode_dot(form, data, table):
    upper = table.astype(jnp.bfloat16)
    lower = (table - upper.astype(jnp.float32)).astype(jnp.bfloat16)
    first = jnp.einsum(form, data, upper, preferred_element_type=jnp.float32)
    return first + jnp.einsum(form, data, lower, preferred_element_type=jnp.float32)


def body(field, cotangent, spectral_weight, bypass_weight):
    cells_x = field.shape[1]
    cells_y = field.shape[2]
    channels = field.shape[3]
    parts_x = lax.axis_size("gx")
    parts_y = lax.axis_size("gy")
    table_x = basis(cells_x * parts_x, MX)
    table_y = basis(cells_y * parts_y, MY)
    table_z = basis(NZ, MZ)
    table_t = basis(NT, MT)
    modes_zt = 4 * MZ * MT
    table_zt = (table_z[:, None, :, None] * table_t[None, :, None, :]).reshape(NZ * NT, modes_zt)

    def analyze(cells):
        matrix = cells.reshape(-1, NZ * NT)
        coeff = mode_dot("rp,pq->rq", matrix, table_zt).astype(jnp.bfloat16)
        coeff = coeff.reshape(cells_x, cells_y, channels, modes_zt)
        along_x = lax.all_to_all(coeff, "gx", split_axis=3, concat_axis=0, tiled=True)
        partial_x = mode_dot("xycq,xk->kycq", along_x, table_x).astype(jnp.bfloat16)
        along_y = lax.all_to_all(partial_x, "gy", split_axis=3, concat_axis=1, tiled=True)
        return mode_dot("kycq,yl->klcq", along_y, table_y).astype(jnp.bfloat16)

    def synthesize(spectrum):
        partial_y = mode_dot("klcq,yl->kycq", spectrum, table_y).astype(jnp.bfloat16)
        returned = lax.all_to_all(partial_y, "gy", split_axis=1, concat_axis=3, tiled=True)
        partial_x = mode_dot("kycq,xk->xycq", returned, table_x).astype(jnp.bfloat16)
        coeff = lax.all_to_all(partial_x, "gx", split_axis=0, concat_axis=3, tiled=True)
        matrix = coeff.reshape(-1, modes_zt)
        values = mode_dot("rq,pq->rp", matrix, table_zt)
        return values.reshape(1, cells_x, cells_y, channels, NZ * NT)

    spectrum = analyze(field)
    mixed = jnp.einsum(
        "klcq,klcoq->kloq", spectrum, spectral_weight, preferred_element_type=jnp.float32
    ).astype(jnp.bfloat16)
    spatial = synthesize(mixed)
    bypass = jnp.einsum("bxyip,io->bxyop", field, bypass_weight, preferred_element_type=jnp.float32)
    pre = spatial + bypass
    unused, pullback = jax.vjp(jax.nn.gelu, pre)
    (slope,) = pullback(cotangent.astype(jnp.float32))
    upstream = slope.astype(jnp.bfloat16)
    bypass_term = jnp.einsum("bxyip,bxyop->io", field, upstream, preferred_element_type=jnp.float32)
    grad_bypass = lax.psum(bypass_term, ("dp", "gx", "gy"))
    spectrum_up = analyze(upstream)
    local_grad = jnp.einsum(
        "klcq,kloq->klcoq", spectrum, spectrum_up, preferred_element_type=jnp.float32
    )
    grad_spectral = lax.psum(local_grad.astype(jnp.bfloat16), "dp").astype(jnp.float32)
    spectrum_back = jnp.einsum(
        "kloq,klcoq->klcq", spectrum_up, spectral_weight, preferred_element_type=jnp.float32
    ).astype(jnp.bfloat16)
    through_bypass = jnp.einsum(
        "bxyop,io->bxyip", upstream, bypass_weight, preferred_element_type=jnp.float32
    )
    grad_field = (synthesize(spectrum_back) + through_bypass).astype(jnp.bfloat16)
    return (grad_field, grad_spectral, grad_bypass)


def solution(mesh):
    in_specs = (
        P("dp", "gx", "gy", None, None),
        P("dp", "gx", "gy", None, None),
        P(None, None, None, None, ("gx", "gy")),
        P(),
    )
    out_specs = (P("dp", "gx", "gy", None, None), P(None, None, None, None, ("gx", "gy")), P())
    return jax.shard_map(body, mesh=mesh, in_specs=in_specs, out_specs=out_specs, check_vma=False)
```

profile of v0, /device:TPU:1, one launch (start us, length us, event | category | flops | bytes accessed | tf_op | source)
XLA Modules:
  0.0 493.5 jit_solution(16601009664940160456)
XLA Ops:
  15.8 6.2 %fusion = (bf16[128,16,24,8]{1,0,3,2:T(8,128)(2,1)}, bf16[128,16,24,8]{1,0,3,2:T(8,128)(2,1)}) fusion(f32[16,8]{0,1:T(8,128)S(1)} %maximum_multiply_fusion.3, f32[128,24]{0,1:T(8,128)S(1)} %maximum_multiply_fusion.2), kind=kLoop, calls=%fused_computation.5 | loop fusion | flops 1966080 | bytes 1585664 | tf_op jit(solution)/shard_map/convert_element_type | solution.py:29
  22.0 11.6 %convert_element_type.256 = bf16[2048,192]{0,1:T(8,128)(2,1)S(1)} reshape(bf16[128,16,24,8]{1,0,3,2:T(8,128)(2,1)} %get-tuple-element.26) | data formatting | bytes 1572864 | tf_op jit(solution)/shard_map/convert_element_type | solution.py:29
  33.7 12.3 %convert_element_type.253 = bf16[2048,192]{0,1:T(8,128)(2,1)} reshape(bf16[128,16,24,8]{1,0,3,2:T(8,128)(2,1)} %get-tuple-element.27) | data formatting | bytes 1572864 | tf_op jit(solution)/shard_map/convert_element_type | solution.py:28
  49.9 5.9 %reshape.160 = bf16[16,2,20,192]{2,1,0,3:T(2,128)(2,1)S(1)} reshape(bf16[640,192]{0,1:T(8,128)(2,1)} %fusion.30) | data formatting | bytes 491520 | tf_op jit(solution)/shard_map/reshape | solution.py:50
  65.0 5.3 %all-to-all-done = bf16[4,2,15360]{2,1,0:T(2,128)(2,1)S(1)} async-done(((bf16[4,2,15360]{2,1,0:T(2,128)(2,1)}), bf16[4,2,15360]{2,1,0:T(2,128)(2,1)S(1)}, u32[]{:S(2)}, u32[]{:S(2)}) %all-to-all-start) | async-done | bytes 245792 | tf_op jit(solution)/shard_map/all_to_all | solution.py:51
  79.3 10.9 %all-to-all-start.1 = ((bf16[16,2,1440]{2,1,0:T(2,128)(2,1)}), bf16[16,2,1440]{2,1,0:T(2,128)(2,1)S(1)}, u32[]{:S(2)}, u32[]{:S(2)}) async-start(bf16[16,2,1440]{2,1,0:T(2,128)(2,1)} %reshape.164), calls=%async_computation.1 | async-start | bytes 196608 | tf_op jit(solution)/shard_map/all_to_all | solution.py:53
  90.4 8.2 %all-to-all-done.1 = bf16[16,2,1440]{2,1,0:T(2,128)(2,1)S(1)} async-done(((bf16[16,2,1440]{2,1,0:T(2,128)(2,1)}), bf16[16,2,1440]{2,1,0:T(2,128)(2,1)S(1)}, u32[]{:S(2)}, u32[]{:S(2)}) %all-to-all-start.1) | async-done | bytes 92192 | tf_op jit(solution)/shard_map/all_to_all | solution.py:53
  101.2 5.0 %multiply_reduce_fusion.1 = bf16[24,24,3,20]{1,0,2,3:T(8,128)(2,1)S(1)} fusion(f32[24,24,3,20]{1,0,2,3:T(8,128)S(1)} %copy.223, bf16[24,24,20,20,3]{1,0,4,3,2:T(8,128)(2,1)} %param.6), kind=kLoop, calls=%fused_computation.3 | loop fusion | flops 2039040 | bytes 1589760 | tf_op jit(solution)/shard_map/klcq,klcoq->kloq/dot_general | solution.py:66
  107.7 10.9 %all_to_all.138 = bf16[16,2,1440]{2,1,0:T(2,128)(2,1)S(1)} all-to-all(bf16[16,2,1440]{2,1,0:T(2,128)(2,1)S(1)} %reshape.166), channel_id=1, replica_groups=mesh['dp'=4,'gx'=4,'gy'=16] {'gy'}, dimensions={0} | all-to-all | bytes 184320 | tf_op jit(solution)/shard_map/all_to_all | solution.py:58
  122.3 9.6 %all_to_all.139 = bf16[4,2,15360]{2,1,0:T(2,128)(2,1)S(1)} all-to-all(bf16[4,2,15360]{2,1,0:T(2,128)(2,1)S(1)} %reshape.168), channel_id=1, replica_groups=mesh['dp'=4,'gx'=4,'gy'=16] {'gx'}, dimensions={0} | all-to-all | bytes 491520 | tf_op jit(solution)/shard_map/all_to_all | solution.py:60
  139.5 6.7 %reshape.142 = f32[1,16,2,20,2048]{4,3,2,1,0:T(8,128)} reshape(f32[640,2048]{1,0:T(8,128)} %convolution_add_fusion.1) | data formatting | bytes 10485760 | tf_op jit(solution)/shard_map/reshape | solution.py:63
  146.1 11.0 %fusion.4 = bf16[1,16,2,20,2048]{4,3,2,1,0:T(8,128)(2,1)} fusion(f32[1,16,2,20,2048]{4,3,2,1,0:T(8,128)} %reshape.142, bf16[1,16,2,20,2048]{4,2,3,1,0:T(2,128)(2,1)} %param.5, bf16[16,2,20,2048]{3,1,2,0:T(2,128)(2,1)} %bitcast.208, bf16[20,20]{1,0:T(8,128)(2,1)S(1)} %copy-done), kind=kOutput, calls=%fused_computation.13 | convolution fusion | flops 81264640 | bytes 13108000 | tf_op jit(solution)/shard_map/bxyip,io->bxyop/dot_general | solution.py:70
  157.1 5.3 %reshape.144 = bf16[640,2048]{1,0:T(8,128)(2,1)} reshape(bf16[1,16,2,20,2048]{4,3,2,1,0:T(8,128)(2,1)} %fusion.4) | data formatting | bytes 5242880 | tf_op jit(solution)/shard_map/reshape | solution.py:48
  175.3 8.8 %all_to_all.140 = bf16[4,2,15360]{2,1,0:T(2,128)(2,1)} all-to-all(bf16[4,2,15360]{2,1,0:T(2,128)(2,1)S(1)} %reshape.170), channel_id=1, replica_groups=mesh['dp'=4,'gx'=4,'gy'=16] {'gx'}, dimensions={0} | all-to-all | bytes 491520 | tf_op jit(solution)/shard_map/all_to_all | solution.py:51
  184.2 6.0 %reshape.171 = bf16[192,16,2,20]{3,2,1,0:T(2,128)(2,1)S(1)} reshape(bf16[4,2,15360]{2,1,0:T(2,128)(2,1)} %all_to_all.140) | data formatting | bytes 491520
  196.9 5.2 %all-to-all-start.5 = ((bf16[16,2,1440]{2,1,0:T(2,128)(2,1)}), bf16[16,2,1440]{2,1,0:T(2,128)(2,1)S(1)}, u32[]{:S(2)}, u32[]{:S(2)}) async-start(bf16[16,2,1440]{2,1,0:T(2,128)(2,1)} %reshape.172), calls=%async_computation.5 | async-start | bytes 196608 | tf_op jit(solution)/shard_map/all_to_all | solution.py:53
  204.3 6.3 %all-to-all-done.5 = bf16[16,2,1440]{2,1,0:T(2,128)(2,1)S(1)} async-done(((bf16[16,2,1440]{2,1,0:T(2,128)(2,1)}), bf16[16,2,1440]{2,1,0:T(2,128)(2,1)S(1)}, u32[]{:S(2)}, u32[]{:S(2)}) %all-to-all-start.5) | async-done | bytes 92192 | tf_op jit(solution)/shard_map/all_to_all | solution.py:53
  214.5 5.0 %multiply_reduce_fusion = bf16[24,24,3,20]{1,0,2,3:T(8,128)(2,1)S(1)} fusion(f32[24,24,3,20]{1,0,2,3:T(8,128)S(1)} %copy.224, bf16[24,24,20,20,3]{1,0,4,3,2:T(8,128)(2,1)} %param.6), kind=kLoop, calls=%fused_computation.2 | loop fusion | flops 2039040 | bytes 1589760 | tf_op jit(solution)/shard_map/kloq,klcoq->klcq/dot_general | solution.py:82
  225.3 4.9 fusion.31
  230.2 76.2 %psum.15 = f32[20,20]{0,1:T(8,128)S(1)} all-reduce(f32[20,20]{0,1:T(8,128)S(1)} %fusion.31), channel_id=1, replica_groups=mesh['dp'=4,'gx'=4,'gy'=16] {'dp','gx','gy'}, use_global_device_ids=true, to_apply=%region_1.2 | all-reduce | flops 400 | bytes 3200 | tf_op jit(solution)/shard_map/psum | solution.py:76
  321.4 5.3 %fusion.1 = bf16[24,24,20,20,3]{1,0,4,3,2:T(8,128)(2,1)} fusion(f32[24,24,3,20]{1,0,2,3:T(8,128)S(1)} %copy-done.3, f32[24,24,3,20]{1,0,2,3:T(8,128)} %copy.186), kind=kLoop, calls=%fused_computation.10 | loop fusion | flops 1382400 | bytes 1658880 | tf_op jit(solution)/shard_map/convert_element_type | solution.py:81
  334.4 7.2 %reshape.147 = f32[1,16,2,20,2048]{4,3,2,1,0:T(8,128)} reshape(f32[640,2048]{1,0:T(8,128)} %convolution_add_fusion) | data formatting | bytes 10485760 | tf_op jit(solution)/shard_map/reshape | solution.py:63
  349.9 126.0 %all-reduce.2.cloned.1.call-done = bf16[24,24,20,20,3]{1,0,4,3,2:T(8,128)(2,1)} async-done(((bf16[24,24,20,20,3]{1,0,4,3,2:T(8,128)(2,1)}), bf16[24,24,20,20,3]{1,0,4,3,2:T(8,128)(2,1)}) %all-reduce.2.cloned.1.call-update) | async-done | bytes 1382416 | tf_op jit(solution)/shard_map/psum | solution.py:81
  475.9 10.2 %convert_element_type.284 = f32[24,24,20,20,3]{1,0,4,3,2:T(8,128)} convert(bf16[24,24,20,20,3]{1,0,4,3,2:T(8,128)(2,1)} %all-reduce.2.cloned.1.call-done) | non-fusion elementwise | flops 691200 | bytes 4147200 | tf_op jit(solution)/shard_map/convert_element_type | solution.py:81
  (98 shorter events, 108.3 us)
Async XLA Ops:
  7.2 139.0 %copy-start = (bf16[20,20]{1,0:T(8,128)(2,1)S(1)}, bf16[20,20]{1,0:T(8,128)(2,1)}, u32[]{:S(2)}) copy-start(bf16[20,20]{1,0:T(8,128)(2,1)} %param.7) | copy-start | bytes 2404
  60.0 10.3 %all-to-all-start = ((bf16[4,2,15360]{2,1,0:T(2,128)(2,1)}), bf16[4,2,15360]{2,1,0:T(2,128)(2,1)S(1)}, u32[]{:S(2)}, u32[]{:S(2)}) async-start(bf16[4,2,15360]{2,1,0:T(2,128)(2,1)} %reshape.162), calls=%async_computation | async-start | bytes 491520 | tf_op jit(solution)/shard_map/all_to_all | solution.py:51
  79.3 19.3 %all-to-all-start.1 = ((bf16[16,2,1440]{2,1,0:T(2,128)(2,1)}), bf16[16,2,1440]{2,1,0:T(2,128)(2,1)S(1)}, u32[]{:S(2)}, u32[]{:S(2)}) async-start(bf16[16,2,1440]{2,1,0:T(2,128)(2,1)} %reshape.164), calls=%async_computation.1 | async-start | bytes 196608 | tf_op jit(solution)/shard_map/all_to_all | solution.py:53
  119.1 16.2 %copy-start.1 = (bf16[2048,192]{0,1:T(8,128)(2,1)S(1)}, bf16[2048,192]{0,1:T(8,128)(2,1)}, u32[]{:S(2)}) copy-start(bf16[2048,192]{0,1:T(8,128)(2,1)} %convert_element_type.253) | copy-start | bytes 2359300
  196.9 13.7 %all-to-all-start.5 = ((bf16[16,2,1440]{2,1,0:T(2,128)(2,1)}), bf16[16,2,1440]{2,1,0:T(2,128)(2,1)S(1)}, u32[]{:S(2)}, u32[]{:S(2)}) async-start(bf16[16,2,1440]{2,1,0:T(2,128)(2,1)} %reshape.172), calls=%async_computation.5 | async-start | bytes 196608 | tf_op jit(solution)/shard_map/all_to_all | solution.py:53
  221.6 87.7 %all-to-all-start.6 = ((bf16[16,2,1440]{2,1,0:T(2,128)(2,1)}), bf16[16,2,1440]{2,1,0:T(2,128)(2,1)S(1)}, u32[]{:S(2)}, u32[]{:S(2)}) async-start(bf16[16,2,1440]{2,1,0:T(2,128)(2,1)} %reshape.174), calls=%async_computation.6 | async-start | bytes 196608 | tf_op jit(solution)/shard_map/all_to_all | solution.py:58
  230.2 91.2 %copy-start.3 = (f32[24,24,3,20]{1,0,2,3:T(8,128)S(1)}, f32[24,24,3,20]{1,0,2,3:T(8,128)}, u32[]{:S(2)}) copy-start(f32[24,24,3,20]{1,0,2,3:T(8,128)} %copy.187) | copy-start | bytes 414724
  317.9 9.0 %all-to-all-start.7 = ((bf16[4,2,15360]{2,1,0:T(2,128)(2,1)}), bf16[4,2,15360]{2,1,0:T(2,128)(2,1)S(1)}, u32[]{:S(2)}, u32[]{:S(2)}) async-start(bf16[4,2,15360]{2,1,0:T(2,128)(2,1)} %reshape.176), calls=%async_computation.7 | async-start | bytes 491520 | tf_op jit(solution)/shard_map/all_to_all | solution.py:60
  321.3 154.6 %all-reduce.2.cloned.1.call-start = ((), (), s32[]{:S(2)}) async-start(), calls=%async_computation.8 | async-start | bytes 14745600 | tf_op jit(solution)/shard_map/psum | solution.py:81
  334.4 7.2 %copy-start.2 = (bf16[1,16,2,20,2048]{4,3,2,1,0:T(8,128)(2,1)S(1)}, bf16[1,16,2,20,2048]{4,3,2,1,0:T(8,128)(2,1)}, u32[]{:S(2)}) copy-start(bf16[1,16,2,20,2048]{4,3,2,1,0:T(8,128)(2,1)} %fusion.4) | copy-start | bytes 7864324
Sparse Core Ops, SparseCore 0:
  326.8 149.0 all-reduce.1
where the time goes:
time: 503 us; the launch traced here: 493 us
  waiting for transfers between devices  146 us (29%)
  local copies, waits for them, and re-layouts  120 us (24%)
  blocking collectives  105 us (21%)
  matrix products  46.5 us (9%)
  other arithmetic  32.3 us (6%)
  starting transfers between devices  28 us (6%)
  between operations  15.1 us (3%)
    psum x1, waiting for transfers between devices, body(): lax.psum(local_grad.astype(jnp.bfloat16), 'dp').astype(jnp.float32)  126 us
    psum x1, blocking collectives, body(): grad_bypass = lax.psum(bypass_term, ('dp', 'gx', 'gy'))  76.2 us
    unnamed x29, local copies, waits for them, and re-layouts  39.6 us
    dot_general x12, matrix products, mode_dot(): jnp.einsum(form, data, lower, preferred_element_type=jnp.float32)  16.9 us
    all_to_all x2, starting transfers between devices, analyze(): lax.all_to_all(partial_x, 'gy', split_axis=3, concat_axis=1, tiled=True)  16.1 us
    all_to_all x2, waiting for transfers between devices, analyze(): lax.all_to_all(partial_x, 'gy', split_axis=3, concat_axis=1, tiled=True)  14.5 us
    reshape x2, local copies, waits for them, and re-layouts, synthesize(): return values.reshape(1, cells_x, cells_y, channels, NZ * NT)  13.9 us
    convert_element_type x1, local copies, waits for them, and re-layouts, mode_dot(): upper = table.astype(jnp.bfloat16)  12.3 us
  transfers between devices with their start and end apart: 6, of which 5 were waited for; matrix products, arithmetic and copies ran while one was open for 8% of the time, Pallas kernels for 0%

commit v1 on v0

--- a/solution.py
+++ b/solution.py
@@ -1,3 +1,4 @@
+import functools
 import math
 import jax
 import jax.numpy as jnp
@@ -10,6 +11,40 @@
 MT = 4
 NZ = 128
 NT = 16
+
+
+def attach_threads_here(v0, dimension_no, shard_in):
+    work_now, mat_out = (v0.shape[:dimension_no], v0.shape[dimension_no + 1 :])
+    f_now = v0.reshape(*work_now, shard_in, -1, *mat_out)
+    return jnp.moveaxis(f_now, dimension_no, 0)
+
+
+def search_records(vec, dim_k):
+    passed = list(vec.shape[1:])
+    passed[dim_k] *= vec.shape[0]
+    return jnp.moveaxis(vec, 0, dim_k).reshape(passed)
+
+
+def column_lift(work_x, peer_axis, packet, inner_x):
+    answer = lax.axis_size(peer_axis)
+    small, back = (answer, lax.axis_index(peer_axis))
+    odd = attach_threads_here(work_x, packet, small)
+    rows = [odd[back]]
+    src_i = 1
+    while src_i < small:
+        row_out = odd[back ^ src_i]
+        rows.append(
+            lax.ppermute(
+                row_out, axis_name=peer_axis, perm=[(num, num ^ src_i) for num in range(small)]
+            )
+        )
+        src_i = src_i + 1
+    all_values = jnp.stack(rows, axis=0)
+    odd = all_values[back ^ jnp.arange(small)]
+    return search_records(odd, inner_x)
+
+
+indices_check = functools.partial(column_lift, peer_axis="gx", packet=3, inner_x=0)
 
 
 def basis(length, kept):
@@ -48,7 +83,7 @@
         matrix = cells.reshape(-1, NZ * NT)
         coeff = mode_dot("rp,pq->rq", matrix, table_zt).astype(jnp.bfloat16)
         coeff = coeff.reshape(cells_x, cells_y, channels, modes_zt)
-        along_x = lax.all_to_all(coeff, "gx", split_axis=3, concat_axis=0, tiled=True)
+        along_x = indices_check(coeff)
         partial_x = mode_dot("xycq,xk->kycq", along_x, table_x).astype(jnp.bfloat16)
         along_y = lax.all_to_all(partial_x, "gy", split_axis=3, concat_axis=1, tiled=True)
         return mode_dot("kycq,yl->klcq", along_y, table_y).astype(jnp.bfloat16)

time: 503 us -> 481 us (0.956)
  local copies, waits for them, and re-layouts: 120 us -> 92.5 us
  waiting for transfers between devices: 146 us -> 157 us
  blocking collectives: 105 us -> 97.3 us
    unnamed x29 -> x25, local copies, waits for them, and re-layouts: 39.6 us -> 22 us
    ppermute x0 -> x6, waiting for transfers between devices: none -> 17.1 us  [column_lift(): lax.ppermute(row_out, axis_name=peer_axis, perm=[(num, num ^ src_i) for n...]
    reshape x2 -> x0, local copies, waits for them, and re-layouts: 9.73 us -> none  [analyze(): coeff = coeff.reshape(cells_x, cells_y, channels, modes_zt)]
    ppermute x0 -> x6, starting transfers between devices: none -> 9.25 us  [column_lift(): lax.ppermute(row_out, axis_name=peer_axis, perm=[(num, num ^ src_i) for n...]
    all_to_all x1 -> x0, blocking collectives: 8.85 us -> none  [analyze(): lax.all_to_all(coeff, 'gx', split_axis=3, concat_axis=0, tiled=True)]
    all_to_all x4 -> x0, local copies, waits for them, and re-layouts: 7.39 us -> none  [analyze(): lax.all_to_all(coeff, 'gx', split_axis=3, concat_axis=0, tiled=True)]
    all_to_all x1 -> x0, waiting for transfers between devices: 5.29 us -> none  [analyze(): lax.all_to_all(coeff, 'gx', split_axis=3, concat_axis=0, tiled=True)]
  transfers between devices with their start and end apart: 6 -> 11, of which waited for: 5 -> 9; matrix products, arithmetic and copies ran while one was open for 8% -> 8% of each run, Pallas kernels for 0% -> 0%
where the time goes in v1:
time: 481 us; the launch traced here: 471 us
  waiting for transfers between devices  157 us (33%)
  blocking collectives  97.3 us (20%)
  local copies, waits for them, and re-layouts  92.5 us (19%)
  matrix products  46.5 us (10%)
  other arithmetic  32.7 us (7%)
  starting transfers between devices  30.6 us (6%)
  between operations  14.9 us (3%)
    psum x1, waiting for transfers between devices, body(): lax.psum(local_grad.astype(jnp.bfloat16), 'dp').astype(jnp.float32)  125 us
    psum x1, blocking collectives, body(): grad_bypass = lax.psum(bypass_term, ('dp', 'gx', 'gy'))  77.1 us
    unnamed x25, local copies, waits for them, and re-layouts  22 us
    ppermute x6, waiting for transfers between devices, column_lift(): lax.ppermute(row_out, axis_name=peer_axis, perm=[(num, num ^ src_i) for n...  17.1 us
    dot_general x12, matrix products, mode_dot(): jnp.einsum(form, data, lower, preferred_element_type=jnp.float32)  16.9 us
    all_to_all x2, waiting for transfers between devices, analyze(): lax.all_to_all(partial_x, 'gy', split_axis=3, concat_axis=1, tiled=True)  14.6 us
    all_to_all x2, starting transfers between devices, analyze(): lax.all_to_all(partial_x, 'gy', split_axis=3, concat_axis=1, tiled=True)  14.5 us
    reshape x2, local copies, waits for them, and re-layouts, synthesize(): return values.reshape(1, cells_x, cells_y, channels, NZ * NT)  14.2 us
  transfers between devices with their start and end apart: 11, of which 9 were waited for; matrix products, arithmetic and copies ran while one was open for 8% of the time, Pallas kernels for 0%

profile of v1, /device:TPU:1, one launch (start us, length us, event | category | flops | bytes accessed | tf_op | source)
XLA Modules:
  0.0 471.3 jit_solution(3143538663047896288)
XLA Ops:
  7.5 4.7 copy.116
  15.8 6.2 %fusion = (bf16[128,16,24,8]{1,0,3,2:T(8,128)(2,1)}, bf16[128,16,24,8]{1,0,3,2:T(8,128)(2,1)}) fusion(f32[16,8]{0,1:T(8,128)S(1)} %maximum_multiply_fusion.3, f32[128,24]{0,1:T(8,128)S(1)} %maximum_multiply_fusion.2), kind=kLoop, calls=%fused_computation.7 | loop fusion | flops 1966080 | bytes 1585664 | tf_op jit(solution)/shard_map/convert_element_type | solution.py:64
  22.0 11.6 %convert_element_type.256 = bf16[2048,192]{0,1:T(8,128)(2,1)S(1)} reshape(bf16[128,16,24,8]{1,0,3,2:T(8,128)(2,1)} %get-tuple-element.31) | data formatting | bytes 1572864 | tf_op jit(solution)/shard_map/convert_element_type | solution.py:64
  33.7 12.3 %convert_element_type.253 = bf16[2048,192]{0,1:T(8,128)(2,1)} reshape(bf16[128,16,24,8]{1,0,3,2:T(8,128)(2,1)} %get-tuple-element.32) | data formatting | bytes 1572864 | tf_op jit(solution)/shard_map/convert_element_type | solution.py:63
  58.2 6.4 %collective-permute-done.1 = bf16[16,2,20,48]{3,0,2,1:T(8,128)(2,1)S(1)} collective-permute-done((bf16[16,2,20,48]{3,0,2,1:T(8,128)(2,1)S(1)}, bf16[16,2,20,48]{3,0,2,1:T(8,128)(2,1)S(1)}, u32[]{:S(2)}, u32[]{:S(2)}) %collective-permute-start.1) | collective-permute-done | bytes 61472 | tf_op jit(solution)/shard_map/ppermute | solution.py:37
  70.7 9.8 %all-to-all-start = ((bf16[16,2,1440]{2,1,0:T(2,128)(2,1)}), bf16[16,2,1440]{2,1,0:T(2,128)(2,1)S(1)}, u32[]{:S(2)}, u32[]{:S(2)}) async-start(bf16[16,2,1440]{2,1,0:T(2,128)(2,1)} %reshape.206), calls=%async_computation | async-start | bytes 196608 | tf_op jit(solution)/shard_map/all_to_all | solution.py:88
  80.7 8.3 %all-to-all-done = bf16[16,2,1440]{2,1,0:T(2,128)(2,1)S(1)} async-done(((bf16[16,2,1440]{2,1,0:T(2,128)(2,1)}), bf16[16,2,1440]{2,1,0:T(2,128)(2,1)S(1)}, u32[]{:S(2)}, u32[]{:S(2)}) %all-to-all-start) | async-done | bytes 92192 | tf_op jit(solution)/shard_map/all_to_all | solution.py:88
  91.6 5.0 %multiply_reduce_fusion.1 = bf16[24,24,3,20]{1,0,2,3:T(8,128)(2,1)S(1)} fusion(f32[24,24,3,20]{1,0,2,3:T(8,128)S(1)} %copy.196, bf16[24,24,20,20,3]{1,0,4,3,2:T(8,128)(2,1)} %param.6), kind=kLoop, calls=%fused_computation.5 | loop fusion | flops 2039040 | bytes 1589760 | tf_op jit(solution)/shard_map/klcq,klcoq->kloq/dot_general | solution.py:101
  98.1 10.9 %all_to_all.102 = bf16[16,2,1440]{2,1,0:T(2,128)(2,1)S(1)} all-to-all(bf16[16,2,1440]{2,1,0:T(2,128)(2,1)S(1)} %reshape.208), channel_id=1, replica_groups=mesh['dp'=4,'gx'=4,'gy'=16] {'gy'}, dimensions={0} | all-to-all | bytes 184320 | tf_op jit(solution)/shard_map/all_to_all | solution.py:93
  112.7 9.3 %all_to_all.103 = bf16[4,2,15360]{2,1,0:T(2,128)(2,1)S(1)} all-to-all(bf16[4,2,15360]{2,1,0:T(2,128)(2,1)S(1)} %reshape.210), channel_id=1, replica_groups=mesh['dp'=4,'gx'=4,'gy'=16] {'gx'}, dimensions={0} | all-to-all | bytes 491520 | tf_op jit(solution)/shard_map/all_to_all | solution.py:95
  129.6 6.7 %reshape.172 = f32[1,16,2,20,2048]{4,3,2,1,0:T(8,128)} reshape(f32[640,2048]{1,0:T(8,128)} %convolution_add_fusion.1) | data formatting | bytes 10485760 | tf_op jit(solution)/shard_map/reshape | solution.py:98
  136.3 11.0 %fusion.4 = bf16[1,16,2,20,2048]{4,3,2,1,0:T(8,128)(2,1)} fusion(f32[1,16,2,20,2048]{4,3,2,1,0:T(8,128)} %reshape.172, bf16[1,16,2,20,2048]{4,2,3,1,0:T(2,128)(2,1)} %param.5, bf16[16,2,20,2048]{3,1,2,0:T(2,128)(2,1)} %bitcast.224, bf16[20,20]{1,0:T(8,128)(2,1)S(1)} %copy-done), kind=kOutput, calls=%fused_computation.15 | convolution fusion | flops 81264640 | bytes 13108000 | tf_op jit(solution)/shard_map/bxyip,io->bxyop/dot_general | solution.py:105
  147.3 5.2 %reshape.174 = bf16[640,2048]{1,0:T(8,128)(2,1)} reshape(bf16[1,16,2,20,2048]{4,3,2,1,0:T(8,128)(2,1)} %fusion.4) | data formatting | bytes 5242880 | tf_op jit(solution)/shard_map/reshape | solution.py:83
  165.3 4.2 collective-permute-done.4
  175.5 4.6 all-to-all-start.3
  182.5 6.3 %all-to-all-done.3 = bf16[16,2,1440]{2,1,0:T(2,128)(2,1)S(1)} async-done(((bf16[16,2,1440]{2,1,0:T(2,128)(2,1)}), bf16[16,2,1440]{2,1,0:T(2,128)(2,1)S(1)}, u32[]{:S(2)}, u32[]{:S(2)}) %all-to-all-start.3) | async-done | bytes 92192 | tf_op jit(solution)/shard_map/all_to_all | solution.py:88
  192.6 5.0 %multiply_reduce_fusion = bf16[24,24,3,20]{1,0,2,3:T(8,128)(2,1)S(1)} fusion(f32[24,24,3,20]{1,0,2,3:T(8,128)S(1)} %copy.197, bf16[24,24,20,20,3]{1,0,4,3,2:T(8,128)(2,1)} %param.6), kind=kLoop, calls=%fused_computation.4 | loop fusion | flops 2039040 | bytes 1589760 | tf_op jit(solution)/shard_map/kloq,klcoq->klcq/dot_general | solution.py:117
  203.1 4.9 %fusion.31 = f32[20,20]{0,1:T(8,128)S(1)} fusion(bf16[16,2,20,2048]{3,1,2,0:T(2,128)(2,1)} %bitcast.225, bf16[1,16,2,20,2048]{4,3,2,1,0:T(8,128)(2,1)} %fusion.4), kind=kOutput, calls=%fused_computation.56 | convolution fusion | flops 52428800 | bytes 5244480 | tf_op jit(solution)/shard_map/bxyip,bxyop->io/dot_general | solution.py:110
  208.1 77.1 %psum.15 = f32[20,20]{0,1:T(8,128)S(1)} all-reduce(f32[20,20]{0,1:T(8,128)S(1)} %fusion.31), channel_id=1, replica_groups=mesh['dp'=4,'gx'=4,'gy'=16] {'dp','gx','gy'}, use_global_device_ids=true, to_apply=%region_1.2 | all-reduce | flops 400 | bytes 3200 | tf_op jit(solution)/shard_map/psum | solution.py:111
  300.2 5.3 %fusion.1 = bf16[24,24,20,20,3]{1,0,4,3,2:T(8,128)(2,1)} fusion(f32[24,24,3,20]{1,0,2,3:T(8,128)S(1)} %copy-done.3, f32[24,24,3,20]{1,0,2,3:T(8,128)} %copy.161), kind=kLoop, calls=%fused_computation.12 | loop fusion | flops 1382400 | bytes 1658880 | tf_op jit(solution)/shard_map/convert_element_type | solution.py:116
  313.2 7.5 %reshape.177 = f32[1,16,2,20,2048]{4,3,2,1,0:T(8,128)} reshape(f32[640,2048]{1,0:T(8,128)} %convolution_add_fusion) | data formatting | bytes 10485760 | tf_op jit(solution)/shard_map/reshape | solution.py:98
  324.9 4.2 copy.164
  329.1 125.0 %all-reduce.2.cloned.1.call-done = bf16[24,24,20,20,3]{1,0,4,3,2:T(8,128)(2,1)} async-done(((bf16[24,24,20,20,3]{1,0,4,3,2:T(8,128)(2,1)}), bf16[24,24,20,20,3]{1,0,4,3,2:T(8,128)(2,1)}) %all-reduce.2.cloned.1.call-update) | async-done | bytes 1382416 | tf_op jit(solution)/shard_map/psum | solution.py:116
  454.1 10.2 %convert_element_type.284 = f32[24,24,20,20,3]{1,0,4,3,2:T(8,128)} convert(bf16[24,24,20,20,3]{1,0,4,3,2:T(8,128)(2,1)} %all-reduce.2.cloned.1.call-done) | non-fusion elementwise | flops 691200 | bytes 4147200 | tf_op jit(solution)/shard_map/convert_element_type | solution.py:116
  (119 shorter events, 94.7 us)
Async XLA Ops:
  7.2 129.1 %copy-start = (bf16[20,20]{1,0:T(8,128)(2,1)S(1)}, bf16[20,20]{1,0:T(8,128)(2,1)}, u32[]{:S(2)}) copy-start(bf16[20,20]{1,0:T(8,128)(2,1)} %param.7) | copy-start | bytes 2404
  52.9 5.3 %collective-permute-start = (bf16[16,2,20,48]{3,0,2,1:T(8,128)(2,1)S(1)}, bf16[16,2,20,48]{3,0,2,1:T(8,128)(2,1)S(1)}, u32[]{:S(2)}, u32[]{:S(2)}) collective-permute-start(bf16[16,2,20,48]{3,0,2,1:T(8,128)(2,1)S(1)} %bitcast.252), channel_id=1, source_target_pairs={{0,16},{16,0},{32,48},{48,32},{1,17},{17,1},{33,49},{49,33},{2,18}... | collective-permute-start | bytes 184328 | tf_op jit(solution)/shard_map/ppermute | solution.py:37
  55.1 9.5 %collective-permute-start.1 = (bf16[16,2,20,48]{3,0,2,1:T(8,128)(2,1)S(1)}, bf16[16,2,20,48]{3,0,2,1:T(8,128)(2,1)S(1)}, u32[]{:S(2)}, u32[]{:S(2)}) collective-permute-start(bf16[16,2,20,48]{3,0,2,1:T(8,128)(2,1)S(1)} %bitcast.253), channel_id=1, source_target_pairs={{0,32},{16,48},{32,0},{48,16},{1,33},{17,49},{33,1},{49,17},{2,34}... | collective-permute-start | bytes 184328 | tf_op jit(solution)/shard_map/ppermute | solution.py:37
  57.7 9.9 %collective-permute-start.2 = (bf16[16,2,20,48]{3,0,2,1:T(8,128)(2,1)S(1)}, bf16[16,2,20,48]{3,0,2,1:T(8,128)(2,1)S(1)}, u32[]{:S(2)}, u32[]{:S(2)}) collective-permute-start(bf16[16,2,20,48]{3,0,2,1:T(8,128)(2,1)S(1)} %bitcast.254), channel_id=1, source_target_pairs={{0,48},{16,32},{32,16},{48,0},{1,49},{17,33},{33,17},{49,1},{2,50}... | collective-permute-start | bytes 184328 | tf_op jit(solution)/shard_map/ppermute | solution.py:37
  70.7 18.3 %all-to-all-start = ((bf16[16,2,1440]{2,1,0:T(2,128)(2,1)}), bf16[16,2,1440]{2,1,0:T(2,128)(2,1)S(1)}, u32[]{:S(2)}, u32[]{:S(2)}) async-start(bf16[16,2,1440]{2,1,0:T(2,128)(2,1)} %reshape.206), calls=%async_computation | async-start | bytes 196608 | tf_op jit(solution)/shard_map/all_to_all | solution.py:88
  109.5 16.0 %copy-start.1 = (bf16[2048,192]{0,1:T(8,128)(2,1)S(1)}, bf16[2048,192]{0,1:T(8,128)(2,1)}, u32[]{:S(2)}) copy-start(bf16[2048,192]{0,1:T(8,128)(2,1)} %convert_element_type.253) | copy-start | bytes 2359300
  160.2 5.1 %collective-permute-start.3 = (bf16[16,2,20,48]{3,0,2,1:T(8,128)(2,1)S(1)}, bf16[16,2,20,48]{3,0,2,1:T(8,128)(2,1)S(1)}, u32[]{:S(2)}, u32[]{:S(2)}) collective-permute-start(bf16[16,2,20,48]{3,0,2,1:T(8,128)(2,1)S(1)} %bitcast.257), channel_id=1, source_target_pairs={{0,16},{16,0},{32,48},{48,32},{1,17},{17,1},{33,49},{49,33},{2,18}... | collective-permute-start | bytes 184328 | tf_op jit(solution)/shard_map/ppermute | solution.py:37
  160.6 8.9 %collective-permute-start.4 = (bf16[16,2,20,48]{3,0,2,1:T(8,128)(2,1)S(1)}, bf16[16,2,20,48]{3,0,2,1:T(8,128)(2,1)S(1)}, u32[]{:S(2)}, u32[]{:S(2)}) collective-permute-start(bf16[16,2,20,48]{3,0,2,1:T(8,128)(2,1)S(1)} %bitcast.256), channel_id=1, source_target_pairs={{0,32},{16,48},{32,0},{48,16},{1,33},{17,49},{33,1},{49,17},{2,34}... | collective-permute-start | bytes 184328 | tf_op jit(solution)/shard_map/ppermute | solution.py:37
  162.4 10.0 %collective-permute-start.5 = (bf16[16,2,20,48]{3,0,2,1:T(8,128)(2,1)S(1)}, bf16[16,2,20,48]{3,0,2,1:T(8,128)(2,1)S(1)}, u32[]{:S(2)}, u32[]{:S(2)}) collective-permute-start(bf16[16,2,20,48]{3,0,2,1:T(8,128)(2,1)S(1)} %bitcast.255), channel_id=1, source_target_pairs={{0,48},{16,32},{32,16},{48,0},{1,49},{17,33},{33,17},{49,1},{2,50}... | collective-permute-start | bytes 184328 | tf_op jit(solution)/shard_map/ppermute | solution.py:37
  175.5 13.2 %all-to-all-start.3 = ((bf16[16,2,1440]{2,1,0:T(2,128)(2,1)}), bf16[16,2,1440]{2,1,0:T(2,128)(2,1)S(1)}, u32[]{:S(2)}, u32[]{:S(2)}) async-start(bf16[16,2,1440]{2,1,0:T(2,128)(2,1)} %reshape.212), calls=%async_computation.3 | async-start | bytes 196608 | tf_op jit(solution)/shard_map/all_to_all | solution.py:88
  199.7 88.4 %all-to-all-start.4 = ((bf16[16,2,1440]{2,1,0:T(2,128)(2,1)}), bf16[16,2,1440]{2,1,0:T(2,128)(2,1)S(1)}, u32[]{:S(2)}, u32[]{:S(2)}) async-start(bf16[16,2,1440]{2,1,0:T(2,128)(2,1)} %reshape.214), calls=%async_computation.4 | async-start | bytes 196608 | tf_op jit(solution)/shard_map/all_to_all | solution.py:93
  208.1 92.1 %copy-start.3 = (f32[24,24,3,20]{1,0,2,3:T(8,128)S(1)}, f32[24,24,3,20]{1,0,2,3:T(8,128)}, u32[]{:S(2)}) copy-start(f32[24,24,3,20]{1,0,2,3:T(8,128)} %copy.162) | copy-start | bytes 414724
  296.7 9.0 %all-to-all-start.5 = ((bf16[4,2,15360]{2,1,0:T(2,128)(2,1)}), bf16[4,2,15360]{2,1,0:T(2,128)(2,1)S(1)}, u32[]{:S(2)}, u32[]{:S(2)}) async-start(bf16[4,2,15360]{2,1,0:T(2,128)(2,1)} %reshape.216), calls=%async_computation.5 | async-start | bytes 491520 | tf_op jit(solution)/shard_map/all_to_all | solution.py:95
  300.1 153.9 %all-reduce.2.cloned.1.call-start = ((), (), s32[]{:S(2)}) async-start(), calls=%async_computation.6 | async-start | bytes 14745600 | tf_op jit(solution)/shard_map/psum | solution.py:116
  313.2 7.5 %copy-start.2 = (bf16[1,16,2,20,2048]{4,3,2,1,0:T(8,128)(2,1)S(1)}, bf16[1,16,2,20,2048]{4,3,2,1,0:T(8,128)(2,1)}, u32[]{:S(2)}) copy-start(bf16[1,16,2,20,2048]{4,3,2,1,0:T(8,128)(2,1)} %fusion.4) | copy-start | bytes 7864324
Sparse Core Ops, SparseCore 0:
  305.7 148.3 all-reduce.1
